TPU v7x, 256 devices: a whole 4x4x8 slice. The times are simulated.
256 devices in a mesh: dp: 4 (over y_lo, core), row: 8 (over z), col: 8 (over y_hi, x).
Axes of the slice: x: 4, y: 4 (y_hi: 2, y_lo: 2; y = y_hi * 2 + y_lo), z: 8, core: 2. Of those that a mesh axis runs over, the one named last changes fastest.
Arguments:
- hidden: bfloat16 [4096, 28672], P(('dp', 'col'), 'row'), may hold values from -6 to 6
- codes: bfloat16 [28672, 4096], P('row', 'col'), may hold values from -1 to 1
- scales: float32 [224, 32], P('row', 'col'), may hold values from 0.004 to 0.016
- out_grad: bfloat16 [4096, 4096], P(('dp', 'row'), 'col'), may hold values from -6 to 6
Outputs:
- output: bfloat16 [4096, 4096], P(('dp', 'row'), 'col')
- input_grad: bfloat16 [4096, 28672], P(('dp', 'col'), 'row')
- weight_grad: float32 [28672, 4096], P(('row', 'dp'), 'col')
All inputs are finite; a program needn't handle non-finite values.
Results may differ from a plain program's by a relative error of at most 0.0049.
Values may be sent and summed in bfloat16 or wider, within the bound.
A program may use at most 128 MiB of HBM per device.

v0:
```python
import math

import jax
import jax.numpy as jnp
from jax import lax
from jax.sharding import PartitionSpec as P


def dequantize(codes, scales, side):
    rows, cols = codes.shape
    blocks = codes.astype(jnp.float32).reshape(rows // side, side, cols // side, side)
    blocks = blocks * scales[:, None, :, None]
    return blocks.reshape(rows, cols).astype(jnp.bfloat16)


def per_device(hidden, codes, scales, out_grad):
    side = codes.shape[0] // scales.shape[0]
    weight = dequantize(codes, scales, side)
    group_rows = lax.all_gather(hidden, "col", axis=0, tiled=True)
    tokens_group = group_rows.shape[0]
    piece = group_rows
    output = lax.psum_scatter(
        jnp.dot(piece, weight, preferred_element_type=jnp.float32),
        "row",
        scatter_dimension=0,
        tiled=True,
    ).astype(jnp.bfloat16)
    group_cot = lax.all_gather(out_grad, "row", axis=0, tiled=True)
    piece = group_cot
    input_grad = lax.psum_scatter(
        lax.dot_general(
            piece, weight, (((1,), (1,)), ((), ())), preferred_element_type=jnp.float32
        ),
        "col",
        scatter_dimension=0,
        tiled=True,
    ).astype(jnp.bfloat16)
    factor = 1.0 / math.sqrt(tokens_group * lax.axis_size("dp"))
    piece = group_rows
    summed = lax.psum_scatter(
        lax.dot_general(
            piece, group_cot, (((0,), (0,)), ((), ())), preferred_element_type=jnp.float32
        ),
        "dp",
        scatter_dimension=0,
        tiled=True,
    )
    return (output, input_grad, summed * factor)


def solution(mesh):
    in_specs = (P(("dp", "col"), "row"), P("row", "col"), P("row", "col"), P(("dp", "row"), "col"))
    out_specs = (P(("dp", "row"), "col"), P(("dp", "col"), "row"), P(("row", "dp"), "col"))
    return jax.shard_map(
        per_device, mesh=mesh, in_specs=in_specs, out_specs=out_specs, check_vma=False
    )
```

profile of v0, /device:TPU:25, one launch (start us, length us, event | category | flops | bytes accessed | tf_op | source)
XLA Modules:
  0.0 461.6 jit_solution(17695888232489027427)
XLA Ops:
  7.2 0.0 all-gather.3.cloned.1.call-start
  7.2 0.7 all-gather.3.cloned.1.call-update
  7.9 0.0 all-gather.5.cloned.1.call-start
  7.9 0.7 all-gather.5.cloned.1.call-update
  8.6 0.0 reduce-scatter.4.cloned.1.call-start
  8.7 0.8 copy.7
  9.5 106.2 %all-gather.3.cloned.1.call-done = bf16[1024,3584]{1,0:T(8,128)(2,1)} async-done(((bf16[128,3584]{1,0:T(8,128)(2,1)}), bf16[1024,3584]{1,0:T(8,128)(2,1)}) %all-gather.3.cloned.1.call-update) | async-done | bytes 7340048 | tf_op jit(solution)/shard_map/all_gather | solution.py:19
  115.7 1.0 mul.17
  116.7 2.9 copy-done
  119.7 7.7 %convolution_bitcast_fusion.1 = f32[1024,512]{0,1:T(8,128)} fusion(bf16[1024,3584]{1,0:T(8,128)(2,1)} %all-gather.3.cloned.1.call-done, f32[448,8,4,128]{3,2,1,0:T(4,128)S(1)} %bitcast.16, bf16[3584,512]{1,0:T(8,128)(2,1)S(1)} %copy-done.1), kind=kOutput, calls=%fused_computation.3 | convolution fusion | flops 3763601408 | bytes 20447232 | tf_op jit(solution)/shard_map/dot_general | solution.py:23
  127.4 0.0 reduce-scatter.8.cloned.1.call-start
  127.5 23.7 %all-gather.5.cloned.1.call-done = bf16[1024,512]{1,0:T(8,128)(2,1)} async-done(((bf16[128,512]{1,0:T(8,128)(2,1)}), bf16[1024,512]{1,0:T(8,128)(2,1)}) %all-gather.5.cloned.1.call-update) | async-done | bytes 1048592 | tf_op jit(solution)/shard_map/all_gather | solution.py:28
  151.1 10.2 %fusion.3 = f32[3584,512]{1,0:T(8,128)} fusion(bf16[1024,3584]{1,0:T(8,128)(2,1)} %all-gather.3.cloned.1.call-done, bf16[1024,512]{1,0:T(8,128)(2,1)} %all-gather.5.cloned.1.call-done), kind=kOutput, calls=%fused_computation.5 | convolution fusion | flops 3758096384 | bytes 15728640 | tf_op jit(solution)/shard_map/dot_general | solution.py:41
  161.4 0.0 reduce-scatter.6.cloned.1.call-start
  161.4 1.1 copy-done.2
  162.6 11.4 %convolution_bitcast_fusion = f32[1024,3584]{0,1:T(8,128)} fusion(bf16[1024,512]{1,0:T(8,128)(2,1)S(1)} %copy-done.2, f32[448,8,4,128]{3,2,1,0:T(4,128)} %bitcast.17, bf16[3584,512]{1,0:T(8,128)(2,1)} %param.5), kind=kOutput, calls=%fused_computation | convolution fusion | flops 3763601408 | bytes 26738688 | tf_op jit(solution)/shard_map/dot_general | solution.py:31
  174.1 21.2 %reduce-scatter.4.cloned.1.call-done = f32[128,512]{0,1:T(8,128)} async-done(((f32[1024,512]{0,1:T(8,128)}), f32[128,512]{0,1:T(8,128)}) %reduce-scatter.4.cloned.1.call-update) | async-done | bytes 262160 | tf_op jit(solution)/shard_map/reduce_scatter | solution.py:22
  195.2 1.0 convert_element_type.14
  196.2 0.8 copy.8
  197.0 76.9 %reduce-scatter.8.cloned.1.call-done = f32[896,512]{1,0:T(8,128)} async-done(((f32[3584,512]{1,0:T(8,128)}), f32[896,512]{1,0:T(8,128)}) %reduce-scatter.8.cloned.1.call-update) | async-done | bytes 1835024 | tf_op jit(solution)/shard_map/reduce_scatter | solution.py:40
  273.9 2.9 broadcast_multiply_fusion
  276.8 175.4 %reduce-scatter.6.cloned.1.call-done = f32[128,3584]{0,1:T(8,128)} async-done(((f32[1024,3584]{0,1:T(8,128)}), f32[128,3584]{0,1:T(8,128)}) %reduce-scatter.6.cloned.1.call-update) | async-done | bytes 1835024 | tf_op jit(solution)/shard_map/reduce_scatter | solution.py:30
  452.2 1.6 convert_element_type.15
  453.8 1.3 copy.9
  (7 shorter events, 0.1 us)
Async XLA Ops:
  7.2 108.5 %all-gather.3.cloned.1.call-start = ((), (), s32[]{:S(2)}) async-start(), calls=%async_computation.3 | async-start | bytes 8257536 | tf_op jit(solution)/shard_map/all_gather | solution.py:19
  7.9 143.2 %all-gather.5.cloned.1.call-start = ((), (), s32[]{:S(2)}) async-start(), calls=%async_computation.5 | async-start | bytes 1179648 | tf_op jit(solution)/shard_map/all_gather | solution.py:28
  8.6 186.6 %reduce-scatter.4.cloned.1.call-start = ((), (), s32[]{:S(2)}) async-start(), calls=%async_computation.4 | async-start | bytes 2359296 | tf_op jit(solution)/shard_map/reduce_scatter | solution.py:22
  115.7 4.0 copy-start.1
  116.7 3.0 copy-start
  127.4 146.5 %reduce-scatter.8.cloned.1.call-start = ((), (), s32[]{:S(2)}) async-start(), calls=%async_computation.7 | async-start | bytes 9175040 | tf_op jit(solution)/shard_map/reduce_scatter | solution.py:40
  161.4 1.2 copy-start.2
  161.4 290.8 %reduce-scatter.6.cloned.1.call-start = ((), (), s32[]{:S(2)}) async-start(), calls=%async_computation.6 | async-start | bytes 16515072 | tf_op jit(solution)/shard_map/reduce_scatter | solution.py:30
Sparse Core Ops, SparseCore 0:
  10.6 105.0 all-gather.2
  117.5 33.5 all-gather.4
  153.7 41.5 reduce-scatter.3
  197.7 76.2 reduce-scatter.7
  278.0 174.2 reduce-scatter.5
where the time goes:
time: 465 us; the launch traced here: 462 us
  waiting for transfers between devices  405 us (87%)
  matrix products  29.4 us (6%)
  between operations  13.8 us (3%)
  local copies, waits for them, and re-layouts  7.93 us (2%)
  other arithmetic  5.48 us (1%)
    reduce_scatter x1, waiting for transfers between devices, per_device(): lax.psum_scatter(lax.dot_general(piece, weight, (((1,), (1,)), ((), ())),...  175 us
    all_gather x1, waiting for transfers between devices, per_device(): group_rows = lax.all_gather(hidden, 'col', axis=0, tiled=True)  106 us
    reduce_scatter x1, waiting for transfers between devices, per_device(): lax.psum_scatter(lax.dot_general(piece, group_cot, (((0,), (0,)), ((), ()...  76.9 us
    all_gather x1, waiting for transfers between devices, per_device(): group_cot = lax.all_gather(out_grad, 'row', axis=0, tiled=True)  23.7 us
    reduce_scatter x1, waiting for transfers between devices, per_device(): lax.psum_scatter(jnp.dot(piece, weight, preferred_element_type=jnp.float3...  21.2 us
    dot_general x1, matrix products, per_device(): lax.dot_general(piece, weight, (((1,), (1,)), ((), ())), preferred_elemen...  11.4 us
    dot_general x1, matrix products, per_device(): lax.dot_general(piece, group_cot, (((0,), (0,)), ((), ())), preferred_ele...  10.2 us
  transfers between devices with their start and end apart: 5, of which 5 were waited for; matrix products, arithmetic and copies ran while one was open for 8% of the time, Pallas kernels for 0%

commit v1 on v0

v1 whole, which is shorter than its diff:
```python
import functools
import math

import jax
import jax.numpy as jnp
from jax import lax
from jax.experimental import pallas as pl
from jax.experimental.pallas import tpu as pltpu
from jax.sharding import PartitionSpec as P

MESH = pl.DeviceIdType.MESH
F32, BF16 = jnp.float32, jnp.bfloat16
NX, NZ = 4, 8
HOPS = {("own", 1): 4, ("own", -1): 3, ("other", 1): 3, ("other", -1): 4}
COPIES = 96


def nt(a, b):
    return lax.dot_general(a, b, (((1,), (1,)), ((), ())), preferred_element_type=F32)


def nn(a, b):
    return lax.dot_general(a, b, (((1,), (0,)), ((), ())), preferred_element_type=F32)


def tn(a, b):
    return lax.dot_general(a, b, (((0,), (0,)), ((), ())), preferred_element_type=F32)


def kernel(
    factor,
    h_ref,
    codes_ref,
    scales_ref,
    g_ref,
    y_out,
    dh_out,
    dw_out,
    codes_own,
    codes_sent,
    w,
    w_sent,
    hg,
    gg,
    dhp,
    dh_r1,
    dh_s2,
    dh_r2,
    dh_sent,
    dh_o,
    yp,
    y_r,
    y_s,
    y_sent,
    y_got,
    y_o,
    dwp,
    dw_s0,
    dw_r0,
    dw_s1,
    dw_r1,
    dw_s2,
    dw_r2,
    dw_o,
    ssem,
    rsem,
    lsem,
):
    tok, quarter = 128, hg.shape[2]
    half = quarter // 2
    dp, z, col = lax.axis_index("dp"), lax.axis_index("row"), lax.axis_index("col")
    yl, c = dp // 2, lax.rem(dp, 2)
    yh, x = col // NX, lax.rem(col, NX)
    oyl, oyh, oc = 1 - yl, 1 - yh, 1 - c

    def dev(x=x, yh=yh, yl=yl, z=z, c=c):
        return {"dp": yl * 2 + c, "row": z, "col": yh * NX + x}

    def xat(o):
        return lax.rem(x + o + NX, NX)

    def zat(o):
        return lax.rem(z + o + 2 * NZ, NZ)

    xto = {1: dev(x=xat(1)), -1: dev(x=xat(-1))}
    zto = {1: dev(z=zat(1)), -1: dev(z=zat(-1))}
    y1, y2, y3 = dev(yl=oyl), dev(yh=oyh), dev(yl=oyl, yh=oyh)
    sib = dev(c=oc)

    def slot_rows(m, n=tok):
        return pl.multiple_of((lax.rem(m, 4) * 2 + m // 4) * tok, tok)

    def xrows(o):
        return pl.multiple_of(xat(o) * (2 * tok), 2 * tok)

    ids = {}
    sends = []

    def key(*k):
        if k not in ids:
            ids[k] = len(ids)
        return ids[k]

    def send(k, src, dst, to):
        i = key(*k)
        copy = pltpu.make_async_remote_copy(
            src_ref=src,
            dst_ref=dst,
            send_sem=ssem.at[i],
            recv_sem=rsem.at[i],
            device_id=to,
            device_id_type=MESH,
        )
        copy.start()
        sends.append(copy)

    def recv(k, dst):
        i = key(*k)
        pltpu.make_async_remote_copy(
            src_ref=dst,
            dst_ref=dst,
            send_sem=ssem.at[i],
            recv_sem=rsem.at[i],
            device_id=sib,
            device_id_type=MESH,
        ).wait_recv()

    local_ids = []

    def local(src, dst):
        i = len(local_ids)
        local_ids.append(i)
        copy = pltpu.make_async_copy(src, dst, lsem.at[i])
        copy.start()
        return copy

    barrier = pltpu.get_barrier_semaphore()
    everyone = [xto[1], xto[-1], zto[1], zto[-1], y1, y2, y3, sib, dev(yl=oyl, yh=oyh, c=oc)]
    for d in everyone:
        pl.semaphore_signal(barrier, inc=1, device_id=d, device_id_type=MESH)
    send_codes = []
    for j in range(2):
        rows = pl.multiple_of((2 * j + oyh) * quarter + c * half, half)
        send_codes.append(local(codes_ref.at[pl.ds(rows, half)], codes_sent.at[j]))
    own_codes = []
    for j in range(2):
        rows = pl.multiple_of((2 * j + yh) * quarter, quarter)
        own_codes.append(local(codes_ref.at[pl.ds(rows, quarter)], codes_own.at[j]))
    grows = slot_rows(z)
    hrows = pl.multiple_of((x * 2 + yh) * tok, tok)
    hrows2 = pl.multiple_of((x * 2 + oyh) * tok, tok)
    own_g = local(g_ref, gg.at[yh, pl.ds(grows, tok)])

    def hcols(j, h):
        return h_ref.at[:, pl.ds(pl.multiple_of((2 * j + h) * quarter, quarter), quarter)]

    own_h = [local(hcols(j, yh), hg.at[j, pl.ds(hrows, tok)]) for j in range(2)]
    pl.semaphore_wait(barrier, len(everyone))

    send(("g2",), g_ref, gg.at[yh, pl.ds(grows, tok)], y2)
    for way in (1, -1):
        send(("g", "own", way, 1), g_ref, gg.at[yh, pl.ds(grows, tok)], zto[way])
    for j in range(2):
        send(("h2", j), hcols(j, oyh), hg.at[j, pl.ds(hrows, tok)], y2)
    for j in range(2):
        for way in (1, -1):
            send(("h", "own", way, j), hcols(j, yh), hg.at[j, pl.ds(hrows, tok)], xto[way])

    unit = 64

    def dequantize(src, dst, q, first):
        def step(u, carry):
            rows = pl.ds(pl.multiple_of(u * unit, unit), unit)
            block = q * (quarter // 128) + (first + u) // 2
            for b in range(dst.shape[1] // 128):
                cols = pl.ds(b * 128, 128)
                tile = src[rows, cols].astype(F32) * scales_ref[block, b]
                dst[rows, cols] = tile.astype(BF16)
            return carry

        lax.fori_loop(0, dst.shape[0] // unit, step, 0)

    def gblock(who):
        return yh if who == "own" else oyh

    def g_hop(who, way, k):
        rows = slot_rows(zat(-k * way))
        place = gg.at[gblock(who), pl.ds(rows, tok)]
        recv(("g", who, way, k), place)
        if k < HOPS[who, way]:
            send(("g", who, way, k + 1), place, place, zto[way])

    for j in range(2):
        send_codes[j].wait()
        dequantize(codes_sent.at[j], w_sent.at[j], 2 * j + oyh, c * (half // unit))
    place = gg.at[oyh, pl.ds(grows, tok)]
    recv(("g2",), place)
    for way in (1, -1):
        send(("g", "other", way, 1), place, place, zto[way])
    for way in (1, -1):
        g_hop("own", way, 1)
    own_codes[0].wait()
    dequantize(codes_own.at[0], w.at[0, yh], yh, 0)
    for way in (1, -1):
        g_hop("other", way, 1)
    for way in (1, -1):
        g_hop("own", way, 2)
    own_codes[1].wait()
    dequantize(codes_own.at[1], w.at[1, yh], 2 + yh, 0)
    for j in range(2):
        place = hg.at[j, pl.ds(hrows2, tok)]
        recv(("h2", j), place)
        for way in (1, -1):
            send(("h", "other", way, j), place, place, xto[way])
    crows = pl.multiple_of(c * half, half)
    ocrows = pl.multiple_of(oc * half, half)
    for j in range(2):
        send(("w3", j), w_sent.at[j], w.at[j, yh, pl.ds(crows, half)], y3)

    def h_pass(who):
        h = gblock(who)
        for way in (1, -1):
            rows = pl.multiple_of((xat(-way) * 2 + h) * tok, tok)
            for j in (0, 1) if way == 1 else (1, 0):
                place = hg.at[j, pl.ds(rows, tok)]
                recv(("h", who, way, j), place)
                if j == (0 if way == 1 else 1):
                    send(("hh", who, way), place, place, xto[way])

    for way in (1, -1):
        g_hop("other", way, 2)
    h_pass("own")
    for k in (3, 4):
        for who in ("own", "other"):
            for way in (1, -1):
                if k <= HOPS[who, way]:
                    g_hop(who, way, k)
    own_g.wait()
    for cp in own_h:
        cp.wait()
    h_pass("other")

    def dest(e):
        return (oyh if e & 2 else yh), (oyl if e & 1 else yl)

    def dw_first(i, carry):
        j, d = i // 2, lax.rem(i, 2)
        total = None
        for o in (0, 1, 3):
            rows = pl.ds(xrows(o), 2 * tok)
            part = tn(hg[j, rows, :], gg[d, rows, :])
            total = part if total is None else total + part
        dwp[j, d] = total
        return carry

    lax.fori_loop(0, 4, dw_first, 0)

    for j in range(2):
        place = w.at[j, oyh, pl.ds(crows, half)]
        recv(("w3", j), place)
        send(("w1", j), place, place, sib)

    def h_last(who):
        h = gblock(who)
        rows = pl.multiple_of((xat(2) * 2 + h) * tok, tok)
        for way in (1, -1):
            recv(("hh", who, way), hg.at[0 if way == 1 else 1, pl.ds(rows, tok)])

    def dh_part(o, j):
        rows = pl.ds(xrows(o), 2 * tok)
        total = nt(gg[0, rows, :], w[j, 0]) + nt(gg[1, rows, :], w[j, 1])
        dhp[j, rows, :] = total.astype(BF16)

    order = ("other", "own")
    for j in range(2):
        recv(("w1", j), w.at[j, oyh, pl.ds(ocrows, half)])
        dh_part(2, j)
        way = 1 if j == 0 else -1
        for i, who in enumerate(order):
            rows = pl.multiple_of((xat(2) * 2 + gblock(who)) * tok, tok)
            send(("dh1", way, who), dhp.at[j, pl.ds(rows, tok)], dh_r1.at[j, i], xto[way])
    for way in (1, -1):
        j = 1 if way == 1 else 0
        dh_part(way, j)
        for i, who in enumerate(order):
            rows = pl.multiple_of((xat(way) * 2 + gblock(who)) * tok, tok)
            send(("dh2", way, who, j), dhp.at[j, pl.ds(rows, tok)], dh_r2.at[0 if way == 1 else 1, j, i], xto[way])

    for who in ("own", "other"):
        h_last(who)
    far = pl.ds(xrows(2), 2 * tok)
    for n, e in enumerate((1, 2, 3, 0)):
        d, j = dest(e)
        dwp[j, d] += tn(hg[j, far, :], gg[d, far, :])
        dw_s0[e] = dwp[j, d, pl.ds(ocrows, half), :].astype(BF16)
        send(("dw0", e), dw_s0.at[e], dw_r0.at[e], sib)

    def dw_sum(e):
        d, j = dest(e)
        recv(("dw0", e), dw_r0.at[e])
        return dwp[j, d, pl.ds(crows, half), :] + dw_r0[e].astype(F32)

    for e in (1, 2):
        dw_s1[e - 1] = dw_sum(e).astype(BF16)
        send(("dw1", e), dw_s1.at[e - 1], dw_r1.at[e - 1], y1)

    for way in (1, -1):
        dh_part(way, 0 if way == 1 else 1)

    def y_part(i, carry):
        d, o = i // NX, lax.rem(i, NX)
        rows = pl.ds(pl.multiple_of(o * (2 * tok), 2 * tok), 2 * tok)
        total = nn(hg[0, rows, :], w[0, d]) + nn(hg[1, rows, :], w[1, d])
        yp[d, rows, :] = total
        return carry

    lax.fori_loop(0, 2 * NX, y_part, 0)
    slots = {}
    for n, k in enumerate((who, way, hop) for (who, way), hops in HOPS.items() for hop in range(1, hops + 1)):
        slots[k] = n

    def y_own(who, o):
        return yp[gblock(who), pl.ds(slot_rows(zat(o)), tok), :]

    def y_hop(who, way, k):
        hops = HOPS[who, way]
        total = y_own(who, way * (hops - k + 1))
        if k > 1:
            before = slots[who, way, k - 1]
            recv(("y", who, way, k - 1), y_r.at[before])
            total = total + y_r[before].astype(F32)
        n = slots[who, way, k]
        y_s[n] = total.astype(BF16)
        send(("y", who, way, k), y_s.at[n], y_r.at[n], zto[way])

    rings = [("other", -1), ("own", 1), ("other", 1), ("own", -1)]
    for who, way in rings:
        y_hop(who, way, 1)

    for i, who in enumerate(order):
        for way in (1, -1):
            j = 0 if way == 1 else 1
            rows = pl.ds(pl.multiple_of((xat(way) * 2 + gblock(who)) * tok, tok), tok)
            recv(("dh1", way, who), dh_r1.at[j, i])
            dh_s2[j, i] = (dhp[j, rows, :].astype(F32) + dh_r1[j, i].astype(F32)).astype(BF16)
            send(("dh2", way, who, j), dh_s2.at[j, i], dh_r2.at[0 if way == 1 else 1, j, i], xto[way])
        for ring in rings:
            y_hop(*ring, 2 + i)
    for j in range(2):
        dh_part(0, j)

    recv(("dw1", 2), dw_r1.at[1])
    dw_s2[0] = ((dw_sum(3) + dw_r1[1].astype(F32)) * factor).astype(BF16)
    third = key("dw3", 0), key("dw3", 1)

    def third_copy(core, to):
        return pltpu.make_async_remote_copy(
            src_ref=dw_s2.at[0],
            dst_ref=dw_r2.at[core],
            send_sem=ssem.at[third[0]],
            recv_sem=rsem.at[third[0] + core],
            device_id=to,
            device_id_type=MESH,
        )

    last = third_copy(c, dev(yl=oyl, yh=oyh, c=yh))
    last.start()
    recv(("dw1", 1), dw_r1.at[0])
    mine = (dw_sum(0) + dw_r1[0].astype(F32)) * factor
    fourth = key("dw4")

    def fourth_copy(core):
        return pltpu.make_async_remote_copy(
            src_ref=dw_s2.at[1],
            dst_ref=dw_r2.at[core],
            send_sem=ssem.at[fourth],
            recv_sem=rsem.at[fourth],
            device_id=sib,
            device_id_type=MESH,
        )

    @pl.when(c == yh)
    def _():
        dw_o[pl.ds(crows, half), :] = mine

    @pl.when(c != yh)
    def _():
        dw_s2[1] = mine.astype(BF16)
        fourth_copy(c).start()

    for who, way in rings:
        if HOPS[who, way] == 4:
            y_hop(who, way, 4)

    def y_total(who):
        total = y_own(who, 0)
        for way in (1, -1):
            n = slots[who, way, HOPS[who, way]]
            recv(("y", who, way, HOPS[who, way]), y_r.at[n])
            total = total + y_r[n].astype(F32)
        return total

    y_sent[...] = y_total("other").astype(BF16)
    send(("y2",), y_sent, y_got, y2)

    outs = []
    total = y_total("own")
    recv(("y2",), y_got)
    y_o[...] = (total + y_got[...].astype(F32)).astype(BF16)
    outs.append(local(y_o, y_out))

    @pl.when(c == yh)
    def _():
        fourth_copy(oc).wait_recv()
        dw_o[pl.ds(ocrows, half), :] = dw_r2[oc].astype(F32)

    @pl.when(c != yh)
    def _():
        for core in range(2):
            third_copy(core, sib).wait_recv()
            dw_o[core * half : (core + 1) * half, :] = dw_r2[core].astype(F32)

    outs.append(local(dw_o, dw_out))

    for i, who in enumerate(order):
        for j in range(2):
            rows = pl.ds(pl.multiple_of((x * 2 + gblock(who)) * tok, tok), tok)
            total = dhp[j, rows, :].astype(F32)
            for n, way in enumerate((1, -1)):
                recv(("dh2", way, who, j), dh_r2.at[n, j, i])
                total = total + dh_r2[n, j, i].astype(F32)
            if who == "own":
                dh_o[2 * j + yh] = total.astype(BF16)
            else:
                dh_sent[j] = total.astype(BF16)
                send(("dh3", j), dh_sent.at[j], dh_o.at[2 * j + yh], y2)
    for j in range(2):
        for h, got in ((yh, False), (oyh, True)):
            q = 2 * j + h
            if got:
                recv(("dh3", j), dh_o.at[q])
            cols = pl.ds(pl.multiple_of(q * quarter, quarter), quarter)
            outs.append(local(dh_o.at[q], dh_out.at[:, cols]))

    for copy in outs:
        copy.wait()
    for copy in sends:
        copy.wait_send()
    last.wait_send()

    @pl.when(c != yh)
    def _():
        fourth_copy(c).wait_send()


def per_device(factor, hidden, codes, scales, out_grad):
    tok, rows = hidden.shape
    cols = codes.shape[1]
    quarter = rows // 4
    half = quarter // 2
    tokens = 8 * tok
    hbm = pl.BlockSpec(memory_space=pl.ANY)
    vmem = pltpu.VMEM
    macs = tokens * rows * cols
    return pl.pallas_call(
        functools.partial(kernel, factor),
        out_shape=(
            jax.ShapeDtypeStruct((tok, cols), BF16),
            jax.ShapeDtypeStruct((tok, rows), BF16),
            jax.ShapeDtypeStruct((quarter, cols), F32),
        ),
        in_specs=[hbm, hbm, pl.BlockSpec(memory_space=pltpu.SMEM), hbm],
        out_specs=(hbm, hbm, hbm),
        scratch_shapes=[
            vmem((2, quarter, cols), BF16),
            vmem((2, half, cols), BF16),
            vmem((2, 2, quarter, cols), BF16),
            vmem((2, half, cols), BF16),
            vmem((2, tokens, quarter), BF16),
            vmem((2, tokens, cols), BF16),
            vmem((2, tokens, quarter), BF16),
            vmem((2, 2, tok, quarter), BF16),
            vmem((2, 2, tok, quarter), BF16),
            vmem((2, 2, 2, tok, quarter), BF16),
            vmem((2, tok, quarter), BF16),
            vmem((4, tok, quarter), BF16),
            vmem((2, tokens, cols), F32),
            vmem((14, tok, cols), BF16),
            vmem((14, tok, cols), BF16),
            vmem((tok, cols), BF16),
            vmem((tok, cols), BF16),
            vmem((tok, cols), BF16),
            vmem((2, 2, quarter, cols), F32),
            vmem((4, half, cols), BF16),
            vmem((4, half, cols), BF16),
            vmem((2, half, cols), BF16),
            vmem((2, half, cols), BF16),
            vmem((2, half, cols), BF16),
            vmem((2, half, cols), BF16),
            vmem((quarter, cols), F32),
            pltpu.SemaphoreType.DMA((COPIES,)),
            pltpu.SemaphoreType.DMA((COPIES,)),
            pltpu.SemaphoreType.DMA((16,)),
        ],
        compiler_params=pltpu.CompilerParams(
            collective_id=0, has_side_effects=True, vmem_limit_bytes=58 * 1024 * 1024
        ),
        cost_estimate=pl.CostEstimate(
            flops=6 * macs, bytes_accessed=16 * tok * rows, transcendentals=0
        ),
    )(hidden, codes, scales, out_grad)


def solution(mesh):
    in_specs = (P(("dp", "col"), "row"), P("row", "col"), P("row", "col"), P(("dp", "row"), "col"))
    out_specs = (P(("dp", "row"), "col"), P(("dp", "col"), "row"), P(("row", "dp"), "col"))

    def step(hidden, codes, scales, out_grad):
        factor = 1.0 / math.sqrt(hidden.shape[0])
        return jax.shard_map(
            functools.partial(per_device, factor),
            mesh=mesh,
            in_specs=in_specs,
            out_specs=out_specs,
            check_vma=False,
        )(hidden, codes, scales, out_grad)

    return step
```

time: 465 us -> 114 us (0.25)
  waiting for transfers between devices: 405 us -> 0 us
  Pallas kernels: 0 us -> 105 us
  matrix products: 29.4 us -> 0 us
  between operations: 13.8 us -> 0.65 us
  other arithmetic: 5.48 us -> 0 us
    reduce_scatter x3 -> x0, waiting for transfers between devices: 274 us -> none  [the longest x1 175 us: per_device(): lax.psum_scatter(lax.dot_general(piece, weight, (((1,), (1,)), ((), ())),...]
    all_gather x2 -> x0, waiting for transfers between devices: 130 us -> none  [the longest x1 106 us: per_device(): group_rows = lax.all_gather(hidden, 'col', axis=0, tiled=True)]
    pallas_call x0 -> x1, Pallas kernels: none -> 105 us  [per_device(): pl.pallas_call(functools.partial(kernel, factor), out_shape=(jax.ShapeDty...]
    dot_general x3 -> x0, matrix products: 29.4 us -> none  [the longest x1 11.4 us: per_device(): lax.dot_general(piece, weight, (((1,), (1,)), ((), ())), preferred_elemen...]
  transfers between devices with their start and end apart: 5 -> 0, of which waited for: 5 -> 0; matrix products, arithmetic and copies ran while one was open for 8% -> 0% of each run, Pallas kernels for 0% -> 0%
where the time goes in v1:
time: 114 us; the launch traced here: 113 us
  Pallas kernels  105 us (92%)
  local copies, waits for them, and re-layouts  6.47 us (6%)
    pallas_call x1, Pallas kernels, per_device(): pl.pallas_call(functools.partial(kernel, factor), out_shape=(jax.ShapeDty...  105 us
    unnamed x6, local copies, waits for them, and re-layouts  6.47 us

profile of v1, /device:TPU:25, one launch (start us, length us, event | category | flops | bytes accessed | tf_op | source)
XLA Modules:
  0.0 112.5 jit_solution(7721983442786935001)
XLA Ops:
  0.6 1.4 %copy.7.scales_ref = f32[28,4]{1,0:T(8,128)} copy(f32[28,4]{0,1:T(4,128)} %param.6) | data formatting | bytes 896 | tf_op args[2]
  2.0 105.4 %shard_map.67 = (bf16[128,512]{1,0:T(8,128)(2,1)}, bf16[128,3584]{1,0:T(8,128)(2,1)}, f32[896,512]{1,0:T(8,128)}) custom-call(bf16[128,3584]{1,0:T(8,128)(2,1)} %h_ref.1, bf16[3584,512]{1,0:T(8,128)(2,1)} %codes_ref.1, f32[28,4]{1,0:T(8,128)} %copy.7.scales_ref, bf16[128,512]{1,0:T(8,128)(2,1)} %g_ref.1), custom_call_target="tpu_custom_call" | custom-call | flops 11274289152 | bytes 7340032 | tf_op jit(solution)/shard_map/pallas_call | solution.py:465
  107.4 0.0 copy-start
  107.4 1.7 %copy.11 = bf16[128,512]{1,0:T(8,128)(2,1)} copy(bf16[128,512]{1,0:T(8,128)(2,1)} %get-tuple-element.6) | data formatting | bytes 262144
  109.1 2.2 %copy.12 = bf16[128,3584]{1,0:T(8,128)(2,1)} copy(bf16[128,3584]{1,0:T(8,128)(2,1)} %get-tuple-element.7) | data formatting | bytes 1835008
  111.3 0.0 copy-done
  111.3 1.2 %copy.13 = f32[896,512]{1,0:T(8,128)} copy(f32[896,512]{1,0:T(8,128)S(1)} %copy-done) | data formatting | bytes 3670016
Async XLA Ops:
  107.4 3.9 %copy-start = (f32[896,512]{1,0:T(8,128)S(1)}, f32[896,512]{1,0:T(8,128)}, u32[]{:S(2)}) copy-start(f32[896,512]{1,0:T(8,128)} %get-tuple-element.8) | copy-start | bytes 5505028

commit v2 on v1

v2 whole, which is shorter than its diff:
```python
import functools
import math

import jax
import jax.numpy as jnp
from jax import lax
from jax.experimental import pallas as pl
from jax.experimental.pallas import tpu as pltpu
from jax.sharding import PartitionSpec as P

MESH = pl.DeviceIdType.MESH
F32, BF16 = jnp.float32, jnp.bfloat16
NX, NZ = 4, 8
HOPS = {("own", 1): 4, ("own", -1): 3, ("other", 1): 3, ("other", -1): 4}
COPIES = 96


def nt(a, b):
    return lax.dot_general(a, b, (((1,), (1,)), ((), ())), preferred_element_type=F32)


def nn(a, b):
    return lax.dot_general(a, b, (((1,), (0,)), ((), ())), preferred_element_type=F32)


def tn(a, b):
    return lax.dot_general(a, b, (((0,), (0,)), ((), ())), preferred_element_type=F32)


def kernel(
    factor,
    h_ref,
    codes_ref,
    scales_hbm,
    g_ref,
    y_out,
    dh_out,
    dw_out,
    scales_ref,
    codes_own,
    codes_sent,
    w,
    w_sent,
    hg,
    gg,
    dhp,
    dh_r1,
    dh_s2,
    dh_r2,
    dh_sent,
    yp,
    y_r,
    y_s,
    y_sent,
    y_got,
    dwp,
    dw_s0,
    dw_r0,
    dw_s1,
    dw_r1,
    dw_s2,
    dw_r2,
    ssem,
    rsem,
    lsem,
):
    tok, quarter = h_ref.shape[0], hg.shape[2]
    half = quarter // 2
    dp, z, col = lax.axis_index("dp"), lax.axis_index("row"), lax.axis_index("col")
    yl, c = dp // 2, lax.rem(dp, 2)
    yh, x = col // NX, lax.rem(col, NX)
    oyl, oyh, oc = 1 - yl, 1 - yh, 1 - c

    def dev(x=x, yh=yh, yl=yl, z=z, c=c):
        return {"dp": yl * 2 + c, "row": z, "col": yh * NX + x}

    def xat(o):
        return lax.rem(x + o + NX, NX)

    def zat(o):
        return lax.rem(z + o + 2 * NZ, NZ)

    xto = {1: dev(x=xat(1)), -1: dev(x=xat(-1))}
    zto = {1: dev(z=zat(1)), -1: dev(z=zat(-1))}
    y1, y2, y3 = dev(yl=oyl), dev(yh=oyh), dev(yl=oyl, yh=oyh)
    sib = dev(c=oc)
    side = {"own": yh, "other": oyh}

    def slot_rows(m):
        return pl.multiple_of((lax.rem(m, 4) * 2 + m // 4) * tok, tok)

    def hslot(o, who):
        return pl.multiple_of((xat(o) * 2 + side[who]) * tok, tok)

    def pair(p):
        return pl.ds(pl.multiple_of(p * (2 * tok), 2 * tok), 2 * tok)

    def first(j, of=yl):
        return of if j == 0 else 1 - of

    ids, sends, outs, local_ids = {}, [], [], []

    def key(*k):
        return ids.setdefault(k, len(ids))

    def send(k, src, dst, to):
        i = key(*k)
        copy = pltpu.make_async_remote_copy(
            src_ref=src,
            dst_ref=dst,
            send_sem=ssem.at[i],
            recv_sem=rsem.at[i],
            device_id=to,
            device_id_type=MESH,
        )
        copy.start()
        sends.append(copy)

    def recv(k, dst):
        i = key(*k)
        pltpu.make_async_remote_copy(
            src_ref=dst,
            dst_ref=dst,
            send_sem=ssem.at[i],
            recv_sem=rsem.at[i],
            device_id=sib,
            device_id_type=MESH,
        ).wait_recv()

    def local(src, dst):
        i = len(local_ids)
        local_ids.append(i)
        copy = pltpu.make_async_copy(src, dst, lsem.at[i])
        copy.start()
        return copy

    barrier = pltpu.get_barrier_semaphore()
    everyone = [xto[1], xto[-1], zto[1], zto[-1], y1, y2, y3, sib, dev(yl=oyl, yh=oyh, c=oc)]
    for d in everyone:
        pl.semaphore_signal(barrier, inc=1, device_id=d, device_id_type=MESH)
    got_scales = local(scales_hbm, scales_ref)
    sent_quarter = [2 * j + oyh for j in range(2)]
    own_quarter = [2 * j + yh for j in range(2)]
    piece = quarter // 4

    def piece_rows(l, core):
        return pl.ds(pl.multiple_of((2 * l + core) * piece, piece), piece)

    crows = pl.multiple_of(c * half, half)
    ocrows = pl.multiple_of(oc * half, half)
    got_sent_codes = [
        local(
            codes_ref.at[pl.ds(pl.multiple_of(sent_quarter[j] * quarter + (2 * oyl + c) * piece, piece), piece)],
            codes_sent.at[j],
        )
        for j in range(2)
    ]
    got_codes = [
        local(codes_ref.at[pl.ds(pl.multiple_of(own_quarter[j] * quarter, quarter), quarter)], codes_own.at[j])
        for j in range(2)
    ]
    grows = pl.ds(slot_rows(z), tok)
    hrows = pl.ds(hslot(0, "own"), tok)
    hrows2 = pl.ds(hslot(0, "other"), tok)
    got_g = local(g_ref, gg.at[yh, grows])

    def cols_of(q):
        return pl.ds(pl.multiple_of(q * quarter, quarter), quarter)

    def hcols(j, h):
        return h_ref.at[:, cols_of(2 * first(j) + h)]

    got_h = [local(hcols(j, yh), hg.at[j, hrows]) for j in range(2)]
    pl.semaphore_wait(barrier, len(everyone))

    send(("g2",), g_ref, gg.at[yh, grows], y2)
    for way in (1, -1):
        send(("h", "own", way, 0), hcols(0, yh), hg.at[0, hrows], xto[way])
    for way in (1, -1):
        send(("g", "own", way, 1), g_ref, gg.at[yh, grows], zto[way])
    send(("h2", 0), hcols(0, oyh), hg.at[0, hrows], y2)
    for way in (1, -1):
        send(("h", "own", way, 1), hcols(1, yh), hg.at[1, hrows], xto[way])
    send(("h2", 1), hcols(1, oyh), hg.at[1, hrows], y2)

    unit = 32

    def dequantize(src, dst, q, start):
        def step(u, carry):
            rows = pl.ds(pl.multiple_of(u * unit, unit), unit)
            block = q * (quarter // 128) + (start + u) // (128 // unit)
            for b in range(dst.shape[1] // 128):
                cols = pl.ds(b * 128, 128)
                tile = src[rows, cols].astype(F32) * scales_ref[b, block]
                dst[rows, cols] = tile.astype(BF16)
            return carry

        lax.fori_loop(0, dst.shape[0] // unit, step, 0)

    def g_hop(who, way, k):
        place = gg.at[side[who], pl.ds(slot_rows(zat(-k * way)), tok)]
        recv(("g", who, way, k), place)
        if k < HOPS[who, way]:
            send(("g", who, way, k + 1), place, place, zto[way])

    def g_hops(who, k):
        for way in (1, -1):
            if k <= HOPS[who, way]:
                g_hop(who, way, k)

    def h_partner(j):
        place = hg.at[j, hrows2]
        for way in (1, -1):
            send(("h", "other", way, j), place, place, xto[way])

    small = tok // 2

    def h_pass(who, j):
        for way in (1, -1):
            row = hslot(-way, who)
            recv(("h", who, way, j), hg.at[j, pl.ds(row, tok)])
            place = hg.at[j, pl.ds(row + (0 if way == 1 else small), small)]
            send(("hh", who, way, j), place, place, xto[way])

    def h_last(who, j):
        row = hslot(2, who)
        for way in (1, -1):
            recv(("hh", who, way, j), hg.at[j, pl.ds(row + (0 if way == 1 else small), small)])

    got_scales.wait()
    for j in range(2):
        got_sent_codes[j].wait()
        dequantize(codes_sent.at[j], w_sent.at[j], sent_quarter[j], (2 * oyl + c) * (piece // unit))
        send(("w3", j), w_sent.at[j], w.at[j, yh, piece_rows(oyl, c)], y3)
    place = gg.at[oyh, grows]
    recv(("g2",), place)
    for way in (1, -1):
        send(("g", "other", way, 1), place, place, zto[way])
    g_hops("own", 1)
    got_codes[0].wait()
    dequantize(codes_own.at[0], w.at[0, yh], own_quarter[0], 0)
    g_hops("other", 1)
    h_pass("own", 0)
    g_hops("own", 2)
    recv(("h2", 0), hg.at[0, hrows2])
    h_partner(0)
    g_hops("other", 2)
    got_codes[1].wait()
    dequantize(codes_own.at[1], w.at[1, yh], own_quarter[1], 0)
    h_pass("own", 1)
    g_hops("own", 3)
    recv(("h2", 1), hg.at[1, hrows2])
    g_hops("other", 3)
    h_pass("other", 0)
    h_partner(1)

    def w_pass(j):
        place = w.at[j, oyh, piece_rows(yl, c)]
        recv(("w3", j), place)
        send(("wy", j), place, place, y1)
        send(("ws", j), place, place, sib)

    def w_relay(j):
        place = w.at[j, oyh, piece_rows(oyl, c)]
        recv(("wy", j), place)
        send(("wt", j), place, place, sib)

    def w_last(j):
        recv(("ws", j), w.at[j, oyh, piece_rows(yl, oc)])
        recv(("wt", j), w.at[j, oyh, piece_rows(oyl, oc)])

    w_pass(0)
    g_hops("own", 4)
    g_hops("other", 4)
    got_g.wait()
    for copy in got_h:
        copy.wait()
    h_last("own", 0)
    h_last("other", 0)

    def dw_part(e):
        j, d = e % 2, side["other" if e & 2 else "own"]
        dwp[j, d] = tn(hg[j], gg[d])
        dw_s0[e] = dwp[j, d, pl.ds(ocrows, half), :].astype(BF16)
        send(("dw0", e), dw_s0.at[e], dw_r0.at[e], sib)

    def dw_sum(e):
        j, d = e % 2, side["other" if e & 2 else "own"]
        recv(("dw0", e), dw_r0.at[e])
        return dwp[j, d, pl.ds(crows, half), :] + dw_r0[e].astype(F32)

    def dw_cross(e):
        dw_s1[e - 1] = dw_sum(e).astype(BF16)
        send(("dw1", e), dw_s1.at[e - 1], dw_r1.at[e - 1], y1)

    def dh_part(o, j):
        rows = pair(xat(o))
        total = nt(gg[0, rows, :], w[j, 0]) + nt(gg[1, rows, :], w[j, 1])
        dhp[j, rows, :] = total.astype(BF16)

    def added(way):
        return 0 if way == 1 else 1

    order = ("other", "own")

    def dh_far(who, way):
        j = added(way)
        send(("dh1", way, who), dhp.at[j, pl.ds(hslot(2, who), tok)], dh_r1.at[j, order.index(who)], xto[way])

    def dh_place(who, way, j):
        return dh_r2.at[0 if way == 1 else 1, j, order.index(who)]

    def dh_near(who, way):
        j = 1 - added(way)
        send(("dh2", way, who, j), dhp.at[j, pl.ds(hslot(way, who), tok)], dh_place(who, way, j), xto[way])

    def dh_add(who, way):
        i, j = order.index(who), added(way)
        recv(("dh1", way, who), dh_r1.at[j, i])
        own = dhp[j, pl.ds(hslot(way, who), tok), :].astype(F32)
        dh_s2[j, i] = (own + dh_r1[j, i].astype(F32)).astype(BF16)
        send(("dh2", way, who, j), dh_s2.at[j, i], dh_place(who, way, j), xto[way])

    def dh_total(who, js=(0, 1)):
        i = order.index(who)
        for j in js:
            total = dhp[j, pl.ds(hslot(0, who), tok), :].astype(F32)
            for n, way in enumerate((1, -1)):
                recv(("dh2", way, who, j), dh_r2.at[n, j, i])
                total = total + dh_r2[n, j, i].astype(F32)
            cols = cols_of(2 * j + yh)
            if who == "own":
                dh_out[:, cols] = total.astype(BF16)
            else:
                dh_sent[j] = total.astype(BF16)
                send(("dh3", j), dh_sent.at[j], dh_out.at[:, cols], y2)

    def y_part(o):
        rows = pair(lax.rem(z + o, NX))

        def step(d, carry):
            yp[d, rows, :] = nn(hg[0, rows, :], w[yl, d]) + nn(hg[1, rows, :], w[oyl, d])
            return carry

        lax.fori_loop(0, 2, step, 0)

    slots = {}
    for n, k in enumerate((who, way, hop) for (who, way), hops in HOPS.items() for hop in range(1, hops + 1)):
        slots[k] = n

    def y_own(who, o):
        return yp[side[who], pl.ds(slot_rows(zat(o)), tok), :]

    def y_hop(who, way, k):
        total = y_own(who, way * (HOPS[who, way] - k + 1))
        if k > 1:
            before = slots[who, way, k - 1]
            recv(("y", who, way, k - 1), y_r.at[before])
            total = total + y_r[before].astype(F32)
        n = slots[who, way, k]
        y_s[n] = total.astype(BF16)
        send(("y", who, way, k), y_s.at[n], y_r.at[n], zto[way])

    def y_hops(k, hops):
        for (who, way), n in HOPS.items():
            if n == hops:
                y_hop(who, way, k)

    third, fourth = key("dw3", 0), key("dw4")
    key("dw3", 1)

    def third_copy(core, to):
        return pltpu.make_async_remote_copy(
            src_ref=dw_s2.at[0],
            dst_ref=dw_r2.at[core],
            send_sem=ssem.at[third],
            recv_sem=rsem.at[third + core],
            device_id=to,
            device_id_type=MESH,
        )

    def fourth_copy(core):
        return pltpu.make_async_remote_copy(
            src_ref=dw_s2.at[1],
            dst_ref=dw_r2.at[core],
            send_sem=ssem.at[fourth],
            recv_sem=rsem.at[fourth],
            device_id=sib,
            device_id_type=MESH,
        )

    def y_total(who):
        total = y_own(who, 0)
        for way in (1, -1):
            n = slots[who, way, HOPS[who, way]]
            recv(("y", who, way, HOPS[who, way]), y_r.at[n])
            total = total + y_r[n].astype(F32)
        return total

    dw_part(2)
    w_pass(1)
    w_relay(0)
    dw_part(0)
    dw_cross(2)
    h_pass("other", 1)
    w_last(0)
    dh_part(2, 0)
    for who in order:
        dh_far(who, 1)
    dh_part(-1, 0)
    for who in order:
        dh_near(who, -1)
    w_relay(1)
    dh_part(1, 0)
    h_last("own", 1)
    h_last("other", 1)
    dw_part(3)
    dw_part(1)
    w_last(1)
    y_part(0)
    y_hops(1, 4)
    dh_part(2, 1)
    for who in order:
        dh_far(who, -1)
    dw_cross(1)
    y_part(3)
    y_hop("other", 1, 1)
    y_part(1)
    y_hop("own", -1, 1)
    y_hops(2, 4)
    recv(("dw1", 2), dw_r1.at[1])
    dw_s2[0] = ((dw_sum(3) + dw_r1[1].astype(F32)) * factor).astype(BF16)
    last = third_copy(c, dev(yl=oyl, yh=oyh, c=yh))
    last.start()
    dh_part(1, 1)
    dh_near("other", 1)
    dh_add("other", 1)
    dh_near("own", 1)
    y_part(2)
    y_hops(2, 3)
    dh_part(-1, 1)
    dh_add("own", 1)
    dh_part(0, 0)
    y_hops(3, 4)
    dh_add("other", -1)
    dh_part(0, 1)
    y_hops(3, 3)
    dh_total("other", (0,))
    dh_add("own", -1)
    y_hops(4, 4)
    recv(("dw1", 1), dw_r1.at[0])
    mine = (dw_sum(0) + dw_r1[0].astype(F32)) * factor

    @pl.when(c == yh)
    def _():
        dw_out[pl.ds(crows, half), :] = mine

    @pl.when(c != yh)
    def _():
        dw_s2[1] = mine.astype(BF16)
        fourth_copy(c).start()

    dh_total("other", (1,))

    @pl.when(c == yh)
    def _():
        fourth_copy(oc).wait_recv()
        dw_out[pl.ds(ocrows, half), :] = dw_r2[oc].astype(F32)

    @pl.when(c != yh)
    def _():
        for core in range(2):
            third_copy(core, sib).wait_recv()
            dw_out[core * half : (core + 1) * half, :] = dw_r2[core].astype(F32)

    y_sent[...] = y_total("other").astype(BF16)
    send(("y2",), y_sent, y_got, y2)
    total = y_total("own")
    recv(("y2",), y_got)
    y_out[...] = (total + y_got[...].astype(F32)).astype(BF16)
    dh_total("own")
    for j in range(2):
        recv(("dh3", j), dh_out.at[:, cols_of(2 * j + oyh)])
    for copy in sends:
        copy.wait_send()
    last.wait_send()

    @pl.when(c != yh)
    def _():
        fourth_copy(c).wait_send()


def per_device(factor, hidden, codes, scales, out_grad):
    tok, rows = hidden.shape
    scales = scales.T
    cols = codes.shape[1]
    quarter = rows // 4
    half = quarter // 2
    tokens = 8 * tok
    hbm = pl.BlockSpec(memory_space=pl.ANY)
    vmem = pltpu.VMEM
    macs = tokens * rows * cols
    return pl.pallas_call(
        functools.partial(kernel, factor),
        out_shape=(
            vmem((tok, cols), BF16),
            vmem((tok, rows), BF16),
            vmem((quarter, cols), F32),
        ),
        in_specs=[hbm] * 4,
        out_specs=(pl.BlockSpec(memory_space=vmem),) * 3,
        scratch_shapes=[
            pltpu.SMEM(scales.shape, F32),
            vmem((2, quarter, cols), BF16),
            vmem((2, quarter // 4, cols), BF16),
            vmem((2, 2, quarter, cols), BF16),
            vmem((2, quarter // 4, cols), BF16),
            vmem((2, tokens, quarter), BF16),
            vmem((2, tokens, cols), BF16),
            vmem((2, tokens, quarter), BF16),
            vmem((2, 2, tok, quarter), BF16),
            vmem((2, 2, tok, quarter), BF16),
            vmem((2, 2, 2, tok, quarter), BF16),
            vmem((2, tok, quarter), BF16),
            vmem((2, tokens, cols), F32),
            vmem((14, tok, cols), BF16),
            vmem((14, tok, cols), BF16),
            vmem((tok, cols), BF16),
            vmem((tok, cols), BF16),
            vmem((2, 2, quarter, cols), F32),
            vmem((4, half, cols), BF16),
            vmem((4, half, cols), BF16),
            vmem((2, half, cols), BF16),
            vmem((2, half, cols), BF16),
            vmem((2, half, cols), BF16),
            vmem((2, half, cols), BF16),
            pltpu.SemaphoreType.DMA((COPIES,)),
            pltpu.SemaphoreType.DMA((COPIES,)),
            pltpu.SemaphoreType.DMA((16,)),
        ],
        compiler_params=pltpu.CompilerParams(
            collective_id=0, has_side_effects=True, vmem_limit_bytes=52 * 1024 * 1024
        ),
        cost_estimate=pl.CostEstimate(
            flops=6 * macs, bytes_accessed=16 * tok * rows, transcendentals=0
        ),
    )(hidden, codes, scales, out_grad)


def solution(mesh):
    in_specs = (P(("dp", "col"), "row"), P("row", "col"), P("row", "col"), P(("dp", "row"), "col"))
    out_specs = (P(("dp", "row"), "col"), P(("dp", "col"), "row"), P(("row", "dp"), "col"))

    def step(hidden, codes, scales, out_grad):
        factor = 1.0 / math.sqrt(hidden.shape[0])
        return jax.shard_map(
            functools.partial(per_device, factor),
            mesh=mesh,
            in_specs=in_specs,
            out_specs=out_specs,
            check_vma=False,
        )(hidden, codes, scales, out_grad)

    return step
```

time: 114 us -> 86 us (0.75)
  the two profiles are of different devices: /device:TPU:25 before, /device:TPU:2 now
where the time goes in v2:
time: 86 us; the launch traced here: 85.9 us
  Pallas kernels  82.4 us (96%)
  local copies, waits for them, and re-layouts  2.81 us (3%)
    pallas_call x1, Pallas kernels, per_device(): pl.pallas_call(functools.partial(kernel, factor), out_shape=(vmem((tok, c...  82.4 us
    unnamed x3, local copies, waits for them, and re-layouts  2.81 us

profile of v2, /device:TPU:2, one launch (start us, length us, event | category | flops | bytes accessed | tf_op | source)
XLA Modules:
  0.0 85.9 jit_solution(9454179481634498417)
XLA Ops:
  0.6 82.4 %shard_map.67 = (bf16[128,512]{1,0:T(8,128)(2,1)S(1)}, bf16[128,3584]{1,0:T(8,128)(2,1)S(1)}, f32[896,512]{1,0:T(8,128)S(1)}) custom-call(bf16[128,3584]{1,0:T(8,128)(2,1)} %h_ref.1, bf16[3584,512]{1,0:T(8,128)(2,1)} %codes_ref.1, f32[4,28]{1,0:T(4,128)} %bitcast.1, bf16[128,512]{1,0:T(8,128)(2,1)} %g_ref.1), custom_call_target="tpu_custom_call" | custom-call | flops 11274289152 | bytes 7340032 | tf_op jit(solution)/shard_map/pallas_call | solution.py:503
  83.1 0.7 copy.10
  83.7 0.9 %copy.11 = bf16[128,3584]{1,0:T(8,128)(2,1)} copy(bf16[128,3584]{1,0:T(8,128)(2,1)S(1)} %get-tuple-element.4) | data formatting | bytes 1835008
  84.6 1.2 %copy.12 = f32[896,512]{1,0:T(8,128)} copy(f32[896,512]{1,0:T(8,128)S(1)} %get-tuple-element.5) | data formatting | bytes 3670016

commit v3 on v2

--- a/solution.py
+++ b/solution.py
@@ -181,7 +181,6 @@
     send(("h2", 0), hcols(0, oyh), hg.at[0, hrows], y2)
     for way in (1, -1):
         send(("h", "own", way, 1), hcols(1, yh), hg.at[1, hrows], xto[way])
-    send(("h2", 1), hcols(1, oyh), hg.at[1, hrows], y2)
 
     unit = 32
 
@@ -232,27 +231,29 @@
         got_sent_codes[j].wait()
         dequantize(codes_sent.at[j], w_sent.at[j], sent_quarter[j], (2 * oyl + c) * (piece // unit))
         send(("w3", j), w_sent.at[j], w.at[j, yh, piece_rows(oyl, c)], y3)
+        if j == 0:
+            send(("h2", 1), hcols(1, oyh), hg.at[1, hrows], y2)
+    for j in range(2):
+        got_codes[j].wait()
+        dequantize(codes_own.at[j], w.at[j, yh], own_quarter[j], 0)
     place = gg.at[oyh, grows]
     recv(("g2",), place)
     for way in (1, -1):
         send(("g", "other", way, 1), place, place, zto[way])
     g_hops("own", 1)
-    got_codes[0].wait()
-    dequantize(codes_own.at[0], w.at[0, yh], own_quarter[0], 0)
+    h_pass("own", 0)
     g_hops("other", 1)
-    h_pass("own", 0)
-    g_hops("own", 2)
     recv(("h2", 0), hg.at[0, hrows2])
     h_partner(0)
+    g_hops("own", 2)
+    h_pass("own", 1)
     g_hops("other", 2)
-    got_codes[1].wait()
-    dequantize(codes_own.at[1], w.at[1, yh], own_quarter[1], 0)
-    h_pass("own", 1)
-    g_hops("own", 3)
-    recv(("h2", 1), hg.at[1, hrows2])
-    g_hops("other", 3)
-    h_pass("other", 0)
-    h_partner(1)
+    def y_rows(who, rows):
+        d = side[who]
+        yp[d, rows, :] = nn(hg[0, rows, :], w[yl, d]) + nn(hg[1, rows, :], w[oyl, d])
+
+    def y_part(o):
+        y_rows("other", pair(lax.rem(z + o, NX)))
 
     def w_pass(j):
         place = w.at[j, oyh, piece_rows(yl, c)]
@@ -269,29 +270,25 @@
         recv(("ws", j), w.at[j, oyh, piece_rows(yl, oc)])
         recv(("wt", j), w.at[j, oyh, piece_rows(oyl, oc)])
 
-    w_pass(0)
-    g_hops("own", 4)
-    g_hops("other", 4)
-    got_g.wait()
-    for copy in got_h:
-        copy.wait()
-    h_last("own", 0)
-    h_last("other", 0)
-
     def dw_part(e):
         j, d = e % 2, side["other" if e & 2 else "own"]
         dwp[j, d] = tn(hg[j], gg[d])
         dw_s0[e] = dwp[j, d, pl.ds(ocrows, half), :].astype(BF16)
         send(("dw0", e), dw_s0.at[e], dw_r0.at[e], sib)
 
-    def dw_sum(e):
+    part = half // 2
+
+    def dw_sum(e, start=0, size=half):
         j, d = e % 2, side["other" if e & 2 else "own"]
+        own = dwp[j, d, pl.ds(pl.multiple_of(crows + start, part), size), :]
+        return own + dw_r0[e, pl.ds(start, size), :].astype(F32)
+
+    def dw_cross(e):
         recv(("dw0", e), dw_r0.at[e])
-        return dwp[j, d, pl.ds(crows, half), :] + dw_r0[e].astype(F32)
-
-    def dw_cross(e):
-        dw_s1[e - 1] = dw_sum(e).astype(BF16)
-        send(("dw1", e), dw_s1.at[e - 1], dw_r1.at[e - 1], y1)
+        for p in range(2):
+            rows = pl.ds(p * part, part)
+            dw_s1[e - 1, rows, :] = dw_sum(e, p * part, part).astype(BF16)
+            send(("dw1", e, p), dw_s1.at[e - 1, rows], dw_r1.at[e - 1, rows], y1)
 
     def dh_part(o, j):
         rows = pair(xat(o))
@@ -335,15 +332,6 @@
                 dh_sent[j] = total.astype(BF16)
                 send(("dh3", j), dh_sent.at[j], dh_out.at[:, cols], y2)
 
-    def y_part(o):
-        rows = pair(lax.rem(z + o, NX))
-
-        def step(d, carry):
-            yp[d, rows, :] = nn(hg[0, rows, :], w[yl, d]) + nn(hg[1, rows, :], w[oyl, d])
-            return carry
-
-        lax.fori_loop(0, 2, step, 0)
-
     slots = {}
     for n, k in enumerate((who, way, hop) for (who, way), hops in HOPS.items() for hop in range(1, hops + 1)):
         slots[k] = n
@@ -361,23 +349,30 @@
         y_s[n] = total.astype(BF16)
         send(("y", who, way, k), y_s.at[n], y_r.at[n], zto[way])
 
-    def y_hops(k, hops):
-        for (who, way), n in HOPS.items():
-            if n == hops:
-                y_hop(who, way, k)
-
-    third, fourth = key("dw3", 0), key("dw4")
-    key("dw3", 1)
-
-    def third_copy(core, to):
+    fourth = key("dw4")
+    third = [key("dw3", n) for n in range(4)][0]
+
+    def third_copy(core, p, to):
+        rows = pl.ds(p * part, part)
         return pltpu.make_async_remote_copy(
-            src_ref=dw_s2.at[0],
-            dst_ref=dw_r2.at[core],
-            send_sem=ssem.at[third],
-            recv_sem=rsem.at[third + core],
+            src_ref=dw_s2.at[0, rows],
+            dst_ref=dw_r2.at[core, rows],
+            send_sem=ssem.at[third + p],
+            recv_sem=rsem.at[third + 2 * p + core],
             device_id=to,
             device_id_type=MESH,
         )
+
+    thirds = []
+
+    def dw_third(p):
+        rows = pl.ds(p * part, part)
+        recv(("dw1", 2, p), dw_r1.at[1, rows])
+        total = dw_sum(3, p * part, part) + dw_r1[1, rows, :].astype(F32)
+        dw_s2[0, rows, :] = (total * factor).astype(BF16)
+        copy = third_copy(c, p, dev(yl=oyl, yh=oyh, c=yh))
+        copy.start()
+        thirds.append(copy)
 
     def fourth_copy(core):
         return pltpu.make_async_remote_copy(
@@ -397,58 +392,85 @@
             total = total + y_r[n].astype(F32)
         return total
 
-    dw_part(2)
+    w_pass(0)
+    g_hops("own", 3)
+    h_pass("other", 0)
+    recv(("h2", 1), hg.at[1, hrows2])
+    h_partner(1)
+    got_g.wait()
+    for copy in got_h:
+        copy.wait()
+    g_hops("other", 3)
+    w_relay(0)
+    g_hops("own", 4)
+    g_hops("other", 4)
     w_pass(1)
-    w_relay(0)
-    dw_part(0)
-    dw_cross(2)
-    h_pass("other", 1)
     w_last(0)
     dh_part(2, 0)
+    dh_part(-1, 0)
+    h_last("own", 0)
+    h_last("other", 0)
+    h_pass("other", 1)
     for who in order:
         dh_far(who, 1)
-    dh_part(-1, 0)
-    for who in order:
-        dh_near(who, -1)
+    dh_near("other", -1)
+    dw_part(2)
+    y_rows("own", pair(x))
+    dw_cross(2)
+    for o in (1, -1):
+        y_rows("own", pair(xat(o)))
     w_relay(1)
-    dh_part(1, 0)
+    dw_part(0)
     h_last("own", 1)
     h_last("other", 1)
     dw_part(3)
+    y_rows("own", pair(xat(2)))
+    y_hop("own", 1, 1)
+    y_hop("own", -1, 1)
+    w_last(1)
+    dh_part(2, 1)
+    dh_far("other", -1)
+    dh_near("own", -1)
     dw_part(1)
-    w_last(1)
     y_part(0)
-    y_hops(1, 4)
-    dh_part(2, 1)
-    for who in order:
-        dh_far(who, -1)
-    dw_cross(1)
+    y_hop("other", -1, 1)
+    dh_part(1, 1)
+    dh_near("other", 1)
     y_part(3)
     y_hop("other", 1, 1)
-    y_part(1)
-    y_hop("own", -1, 1)
-    y_hops(2, 4)
-    recv(("dw1", 2), dw_r1.at[1])
-    dw_s2[0] = ((dw_sum(3) + dw_r1[1].astype(F32)) * factor).astype(BF16)
-    last = third_copy(c, dev(yl=oyl, yh=oyh, c=yh))
-    last.start()
-    dh_part(1, 1)
-    dh_near("other", 1)
+    recv(("dw0", 3), dw_r0.at[3])
+    dw_third(0)
+    dw_cross(1)
+    y_hop("own", 1, 2)
+    y_hop("own", -1, 2)
+    dh_part(1, 0)
     dh_add("other", 1)
     dh_near("own", 1)
+    y_part(1)
+    y_hop("other", -1, 2)
+    dw_third(1)
+    dh_part(-1, 1)
+    dh_add("other", -1)
+    dh_far("own", -1)
     y_part(2)
-    y_hops(2, 3)
-    dh_part(-1, 1)
+    y_hop("other", 1, 2)
+    y_hop("own", 1, 3)
+    y_hop("own", -1, 3)
     dh_add("own", 1)
     dh_part(0, 0)
-    y_hops(3, 4)
-    dh_add("other", -1)
+    y_hop("other", -1, 3)
+    y_hop("other", 1, 3)
     dh_part(0, 1)
-    y_hops(3, 3)
     dh_total("other", (0,))
+    y_hop("own", 1, 4)
+    dh_total("other", (1,))
+    y_hop("other", -1, 4)
     dh_add("own", -1)
-    y_hops(4, 4)
-    recv(("dw1", 1), dw_r1.at[0])
+    y_sent[...] = y_total("other").astype(BF16)
+    send(("y2",), y_sent, y_got, y2)
+    recv(("dw0", 0), dw_r0.at[0])
+    for p in range(2):
+        recv(("dw1", 1, p), dw_r1.at[0, pl.ds(p * part, part)])
     mine = (dw_sum(0) + dw_r1[0].astype(F32)) * factor
 
     @pl.when(c == yh)
@@ -460,8 +482,6 @@
         dw_s2[1] = mine.astype(BF16)
         fourth_copy(c).start()
 
-    dh_total("other", (1,))
-
     @pl.when(c == yh)
     def _():
         fourth_copy(oc).wait_recv()
@@ -470,11 +490,10 @@
     @pl.when(c != yh)
     def _():
         for core in range(2):
-            third_copy(core, sib).wait_recv()
+            for p in range(2):
+                third_copy(core, p, sib).wait_recv()
             dw_out[core * half : (core + 1) * half, :] = dw_r2[core].astype(F32)
 
-    y_sent[...] = y_total("other").astype(BF16)
-    send(("y2",), y_sent, y_got, y2)
     total = y_total("own")
     recv(("y2",), y_got)
     y_out[...] = (total + y_got[...].astype(F32)).astype(BF16)
@@ -483,7 +502,8 @@
         recv(("dh3", j), dh_out.at[:, cols_of(2 * j + oyh)])
     for copy in sends:
         copy.wait_send()
-    last.wait_send()
+    for copy in thirds:
+        copy.wait_send()
 
     @pl.when(c != yh)
     def _():

time: 86 us -> 82.2 us (0.956)
  the two profiles are of different devices: /device:TPU:2 before, /device:TPU:25 now
where the time goes in v3:
time: 82.2 us; the launch traced here: 81.9 us
  Pallas kernels  78.4 us (95%)
  local copies, waits for them, and re-layouts  2.81 us (3%)
    pallas_call x1, Pallas kernels, per_device(): pl.pallas_call(functools.partial(kernel, factor), out_shape=(vmem((tok, c...  78.4 us
    unnamed x3, local copies, waits for them, and re-layouts  2.81 us

profile of v3, /device:TPU:25, one launch (start us, length us, event | category | flops | bytes accessed | tf_op | source)
XLA Modules:
  0.0 81.9 jit_solution(136755960352682739)
XLA Ops:
  0.6 78.4 %shard_map.67 = (bf16[128,512]{1,0:T(8,128)(2,1)S(1)}, bf16[128,3584]{1,0:T(8,128)(2,1)S(1)}, f32[896,512]{1,0:T(8,128)S(1)}) custom-call(bf16[128,3584]{1,0:T(8,128)(2,1)} %h_ref.1, bf16[3584,512]{1,0:T(8,128)(2,1)} %codes_ref.1, f32[4,28]{1,0:T(4,128)} %bitcast.1, bf16[128,512]{1,0:T(8,128)(2,1)} %g_ref.1), custom_call_target="tpu_custom_call" | custom-call | flops 11274289152 | bytes 7340032 | tf_op jit(solution)/shard_map/pallas_call | solution.py:523
  79.1 0.7 copy.10
  79.7 0.9 %copy.11 = bf16[128,3584]{1,0:T(8,128)(2,1)} copy(bf16[128,3584]{1,0:T(8,128)(2,1)S(1)} %get-tuple-element.4) | data formatting | bytes 1835008
  80.7 1.2 %copy.12 = f32[896,512]{1,0:T(8,128)} copy(f32[896,512]{1,0:T(8,128)S(1)} %get-tuple-element.5) | data formatting | bytes 3670016

commit v4 on v3

--- a/solution.py
+++ b/solution.py
@@ -458,10 +458,10 @@
     y_hop("own", -1, 3)
     dh_add("own", 1)
     dh_part(0, 0)
+    dh_part(0, 1)
     y_hop("other", -1, 3)
+    dh_total("other", (0,))
     y_hop("other", 1, 3)
-    dh_part(0, 1)
-    dh_total("other", (0,))
     y_hop("own", 1, 4)
     dh_total("other", (1,))
     y_hop("other", -1, 4)

time: 82.2 us -> 82 us (level)
  no operation moved by 1% of the time
where the time goes in v4:
time: 82 us; the launch traced here: 81.9 us
  Pallas kernels  78.4 us (96%)
  local copies, waits for them, and re-layouts  2.81 us (3%)
    pallas_call x1, Pallas kernels, per_device(): pl.pallas_call(functools.partial(kernel, factor), out_shape=(vmem((tok, c...  78.4 us
    unnamed x3, local copies, waits for them, and re-layouts  2.81 us

profile of v4, /device:TPU:25, one launch (start us, length us, event | category | flops | bytes accessed | tf_op | source)
XLA Modules:
  0.0 81.9 jit_solution(16618697839300771093)
XLA Ops:
  0.6 78.4 %shard_map.67 = (bf16[128,512]{1,0:T(8,128)(2,1)S(1)}, bf16[128,3584]{1,0:T(8,128)(2,1)S(1)}, f32[896,512]{1,0:T(8,128)S(1)}) custom-call(bf16[128,3584]{1,0:T(8,128)(2,1)} %h_ref.1, bf16[3584,512]{1,0:T(8,128)(2,1)} %codes_ref.1, f32[4,28]{1,0:T(4,128)} %bitcast.1, bf16[128,512]{1,0:T(8,128)(2,1)} %g_ref.1), custom_call_target="tpu_custom_call" | custom-call | flops 11274289152 | bytes 7340032 | tf_op jit(solution)/shard_map/pallas_call | solution.py:523
  79.1 0.7 copy.10
  79.7 0.9 %copy.11 = bf16[128,3584]{1,0:T(8,128)(2,1)} copy(bf16[128,3584]{1,0:T(8,128)(2,1)S(1)} %get-tuple-element.4) | data formatting | bytes 1835008
  80.7 1.2 %copy.12 = f32[896,512]{1,0:T(8,128)} copy(f32[896,512]{1,0:T(8,128)S(1)} %get-tuple-element.5) | data formatting | bytes 3670016

commit v5 on v4

--- a/solution.py
+++ b/solution.py
@@ -438,14 +438,14 @@
     dh_near("other", 1)
     y_part(3)
     y_hop("other", 1, 1)
+    dh_part(1, 0)
+    dh_add("other", 1)
+    dh_near("own", 1)
     recv(("dw0", 3), dw_r0.at[3])
     dw_third(0)
     dw_cross(1)
     y_hop("own", 1, 2)
     y_hop("own", -1, 2)
-    dh_part(1, 0)
-    dh_add("other", 1)
-    dh_near("own", 1)
     y_part(1)
     y_hop("other", -1, 2)
     dw_third(1)

time: 82 us -> 82 us (level)
  no operation moved by 1% of the time
where the time goes in v5:
time: 82 us; the launch traced here: 81.9 us
  Pallas kernels  78.4 us (96%)
  local copies, waits for them, and re-layouts  2.81 us (3%)
    pallas_call x1, Pallas kernels, per_device(): pl.pallas_call(functools.partial(kernel, factor), out_shape=(vmem((tok, c...  78.4 us
    unnamed x3, local copies, waits for them, and re-layouts  2.81 us

profile of v5, /device:TPU:25, one launch (start us, length us, event | category | flops | bytes accessed | tf_op | source)
XLA Modules:
  0.0 81.9 jit_solution(445700267897160575)
XLA Ops:
  0.6 78.4 %shard_map.67 = (bf16[128,512]{1,0:T(8,128)(2,1)S(1)}, bf16[128,3584]{1,0:T(8,128)(2,1)S(1)}, f32[896,512]{1,0:T(8,128)S(1)}) custom-call(bf16[128,3584]{1,0:T(8,128)(2,1)} %h_ref.1, bf16[3584,512]{1,0:T(8,128)(2,1)} %codes_ref.1, f32[4,28]{1,0:T(4,128)} %bitcast.1, bf16[128,512]{1,0:T(8,128)(2,1)} %g_ref.1), custom_call_target="tpu_custom_call" | custom-call | flops 11274289152 | bytes 7340032 | tf_op jit(solution)/shard_map/pallas_call | solution.py:523
  79.1 0.7 copy.10
  79.7 0.9 %copy.11 = bf16[128,3584]{1,0:T(8,128)(2,1)} copy(bf16[128,3584]{1,0:T(8,128)(2,1)S(1)} %get-tuple-element.4) | data formatting | bytes 1835008
  80.7 1.2 %copy.12 = f32[896,512]{1,0:T(8,128)} copy(f32[896,512]{1,0:T(8,128)S(1)} %get-tuple-element.5) | data formatting | bytes 3670016
